TPU v7x, 32 devices: a whole 2x2x4 slice. The times are simulated.
32 devices in a mesh: ens: 2 (over y), gx: 16 (over z, x, core).
Axes of the slice: x: 2, y: 2, z: 4, core: 2. Of those that a mesh axis runs over, the one named last changes fastest.
Arguments:
- pressure_prev: float32 [8, 128, 128], P('ens', 'gx'), parts along dimension 0, may hold values from -2.5 to 2.5
- source: float32 [8, 128, 128], P('ens', 'gx'), parts along dimension 0, may hold values from -8 to 8
- permeability: float32 [8, 128, 128], P('ens', 'gx'), parts along dimension 0, may hold values from 0.3 to 3
- region: int32 [8, 128, 128], P('ens', 'gx'), parts along dimension 0, may hold values from 0 to 7
- region_factor: float32 [16], P('ens'), parts along dimension 0, may hold values from 0.3 to 3
- boundary: int32 [8, 128, 128], P('ens', 'gx'), parts along dimension 0, may hold values from 0 to 2
- flux_prev: float32 [3, 8, 128, 128], P(None, 'ens', 'gx'), parts along dimension 1, may hold values from -2 to 2
- concentration: float32 [4, 8, 128, 128], P(None, 'ens', 'gx'), parts along dimension 1, may hold values from 0.2 to 2
- porosity: float32 [8, 128, 128], P('ens', 'gx'), parts along dimension 0, may hold values from 0.3 to 1
- reaction: float32 [8, 4], P('ens'), parts along dimension 0, may hold values from -3 to 3
Outputs:
- pressure: float32 [8, 128, 128], P('ens', 'gx'), parts along dimension 0
- flux_new: float32 [3, 8, 128, 128], P(None, 'ens', 'gx'), parts along dimension 1
- species_new: float32 [4, 8, 128, 128], P(None, 'ens', 'gx'), parts along dimension 1
There are 2 independent parts, one for each index of `ens`. A program takes and returns all parts, laid end to end along the dimension named above; each array names one. Nothing has to cross between parts.
Inputs may be any that keep to these rules, and one draw needn't show every extreme that they name: Index of the cell's material region into region_factor. 0 inner cell, 1 leaky boundary cell, 2 fixed-pressure well cell.
All inputs are finite; a program needn't handle non-finite values.
Results may differ from a plain program's by a relative error of at most 0.0003.
Values sent between devices are 32-bit elements; how exact they have to be, the bound alone decides.
A program may use at most 64 MiB of HBM per device.

v0:
```python
import functools

import jax
import jax.numpy as jnp
from jax import lax
from jax.experimental import pallas as pl
from jax.experimental.pallas import tpu as pltpu
from jax.sharding import PartitionSpec as P

SUBSTEPS = 2
LANES = 128
VMEM_GRANT = 60 * 1024 * 1024
step_size = 0.5


def harmonic(left_val, right_val):
    return 2.0 * left_val * right_val / (left_val + right_val)


def iota(shape, dim):
    return lax.broadcasted_iota(jnp.int32, shape, dim)


def shift_z(field, by):
    zero = jnp.zeros_like(field[:1])
    if by > 0:
        return jnp.concatenate([field[1:], zero], axis=0)
    return jnp.concatenate([zero, field[:-1]], axis=0)


def next_lane(field):
    return pltpu.roll(field, field.shape[-1] - 1, axis=field.ndim - 1)


def last_lane(field):
    return pltpu.roll(field, 1, axis=field.ndim - 1)


def next_row(field):
    return pltpu.roll(field, field.shape[1] - 1, axis=1)


def last_row(field):
    return pltpu.roll(field, 1, axis=1)


def group_transpose(tiles, width):
    count = len(tiles)
    tiles = list(tiles)
    group = iota(tiles[0].shape, 1) // width
    half = count // 2
    while half:
        low = (group & half) == 0
        for i in range(count):
            if i & half:
                continue
            a, b = tiles[i], tiles[i + half]
            tiles[i] = jnp.where(low, a, pltpu.roll(b, half * width, axis=1))
            tiles[i + half] = jnp.where(low, pltpu.roll(a, LANES - half * width, axis=1), b)
        half //= 2
    return tiles


def kernel(
    peers,
    pres_hbm,
    src_hbm,
    perm_hbm,
    region_hbm,
    factor_hbm,
    bound_hbm,
    flux_hbm,
    conc_hbm,
    poro_hbm,
    react_hbm,
    pres_out_hbm,
    flux_out_hbm,
    spec_out_hbm,
    pres_ref,
    src_ref,
    perm_ref,
    region_ref,
    factor_ref,
    bound_ref,
    flux_ref,
    conc_ref,
    poro_ref,
    react_ref,
    load_sem,
    pres_out,
    flux_out,
    spec_out,
    store_sem,
    pack_out,
    pack_in,
    edge_out,
    edge_in,
    turn_out,
    turn_in,
    sum_out,
    sum_in,
    pack_ss,
    pack_rs,
    edge_ss,
    edge_rs,
    turn_ss,
    turn_rs,
    sum_ss,
    sum_rs,
):
    me = lax.axis_index("gx")
    layers, rows, ny = pres_ref.shape
    species_n, _, yrows, nx = conc_ref.shape
    has_low = me > 0
    has_high = me < peers - 1

    barrier = pltpu.get_barrier_semaphore()

    def greet(k, carry):
        pl.semaphore_signal(barrier, inc=1, device_id={"gx": lax.rem(me + k, peers)})
        return carry

    lax.fori_loop(1, peers, greet, 0)

    pairs = (
        (region_hbm, region_ref),
        (factor_hbm, factor_ref),
        (perm_hbm, perm_ref),
        (bound_hbm, bound_ref),
        (pres_hbm, pres_ref),
        (src_hbm, src_ref),
        (flux_hbm, flux_ref),
        (conc_hbm, conc_ref),
        (poro_hbm, poro_ref),
        (react_hbm, react_ref),
    )
    loads = [pltpu.make_async_copy(a, b, load_sem.at[i]) for i, (a, b) in enumerate(pairs)]
    for load in loads:
        load.start()
    for load in loads[:6]:
        load.wait()

    region = region_ref[...]
    factor = jnp.full(region.shape, factor_ref[0], jnp.float32)
    for region_id in range(1, factor_ref.shape[0]):
        factor = jnp.where(region == region_id, factor_ref[region_id], factor)
    conduct = factor * perm_ref[...]
    field = conduct.shape
    row_id = iota(field, 1)
    first_row, end_row = row_id == 0, row_id == rows - 1
    lane_end = iota(field, 2) == ny - 1

    def y_faces(c):
        edge = iota(c.shape, 2) == ny - 1
        return jnp.where(edge, 0.0, harmonic(c, next_lane(c)))

    def z_faces(c):
        zero = jnp.zeros_like(c[:1])
        return jnp.concatenate([harmonic(c[:-1], c[1:]), zero], axis=0)

    ty = y_faces(conduct)
    ty_low = last_lane(ty)
    tz = z_faces(conduct)
    tz_low = shift_z(tz, -1)
    tx = jnp.where(end_row, 0.0, harmonic(conduct, next_row(conduct)))
    tx_low = last_row(tx)
    bound = bound_ref[...]
    leakage = jnp.where(bound == 0, 0.05, jnp.where(bound == 1, 1.0, 10.0)) * conduct
    diag_part = leakage + tx_low + tx + ty_low + ty + tz_low + tz

    def around(f):
        return (
            tx_low * last_row(f)
            + tx * next_row(f)
            + ty_low * last_lane(f)
            + ty * next_lane(f)
            + tz_low * shift_z(f, -1)
            + tz * shift_z(f, 1)
        )

    pres = pres_ref[...]
    res_part = src_ref[...] - (diag_part * pres - around(pres))
    pack_out[0, 0] = conduct[:, 0:1]
    pack_out[0, 1] = pres[:, 0:1]
    pack_out[0, 2] = res_part[:, 0:1]
    pack_out[0, 3] = diag_part[:, 0:1]
    pack_out[0, 4] = res_part[:, 1:2] / diag_part[:, 1:2]
    pack_out[0, 5] = tx[:, 0:1]
    pack_out[1, 0] = conduct[:, rows - 1 : rows]
    pack_out[1, 1] = pres[:, rows - 1 : rows]
    pack_out[1, 2] = res_part[:, rows - 1 : rows]
    pack_out[1, 3] = diag_part[:, rows - 1 : rows]

    pl.semaphore_wait(barrier, peers - 1)

    def to_side(out, into, ss, rs, side):
        return pltpu.make_async_remote_copy(
            src_ref=out,
            dst_ref=into,
            send_sem=ss,
            recv_sem=rs,
            device_id={"gx": me - 1 if side == 0 else me + 1},
        )

    def pack_copy(side):
        used = 6 if side == 0 else 4
        span = pl.ds(0, used)
        return to_side(
            pack_out.at[side, span],
            pack_in.at[1 - side, span],
            pack_ss.at[side],
            pack_rs.at[1 - side],
            side,
        )

    def edge_copy(step, side):
        return to_side(
            edge_out.at[step, side],
            edge_in.at[step, 1 - side],
            edge_ss.at[step, side],
            edge_rs.at[step, 1 - side],
            side,
        )

    def turn_copy(k):
        to = lax.rem(me + k, peers)
        return pltpu.make_async_remote_copy(
            src_ref=turn_out.at[to],
            dst_ref=turn_in.at[me],
            send_sem=turn_ss,
            recv_sem=turn_rs,
            device_id={"gx": to},
        )

    def sum_copy(k):
        to = lax.rem(me + k, peers)
        return pltpu.make_async_remote_copy(
            src_ref=sum_out,
            dst_ref=sum_in.at[me],
            send_sem=sum_ss,
            recv_sem=sum_rs,
            device_id={"gx": to},
        )

    def start_all(copy_of):
        def body(k, carry):
            copy_of(k).start()
            return carry

        lax.fori_loop(1, peers, body, 0)

    def both_sides(copy_of):
        @pl.when(has_low)
        def _():
            copy_of(0).start()

        @pl.when(has_high)
        def _():
            copy_of(1).start()

    def await_sides(copy_of):
        @pl.when(has_low)
        def _():
            copy_of(1).wait_recv()

        @pl.when(has_high)
        def _():
            copy_of(0).wait_recv()

    def sent_sides(copy_of):
        @pl.when(has_low)
        def _():
            copy_of(0).wait_send()

        @pl.when(has_high)
        def _():
            copy_of(1).wait_send()

    def whole(ref_out, ref_in, ss, rs):
        return pltpu.make_async_remote_copy(
            src_ref=ref_out, dst_ref=ref_in, send_sem=ss, recv_sem=rs, device_id={"gx": me}
        )

    both_sides(pack_copy)
    for load in loads[6:]:
        load.wait()
    edge_out[0, 0] = conc_ref[:, :, 0:1, :]
    edge_out[0, 1] = conc_ref[:, :, yrows - 1 : yrows, :]

    flux_y = jnp.where(iota((layers, rows, ny), 2) == ny - 1, 0.0, flux_ref[1])
    flux_y_low = last_lane(flux_y)
    turned = jnp.concatenate([flux_ref[0], flux_y, flux_ref[2], flux_y_low], axis=0)
    turned = turned.reshape(4 * layers * rows, ny).T
    turn_out[...] = turned.reshape(peers, yrows, LANES)
    both_sides(functools.partial(edge_copy, 0))
    start_all(turn_copy)
    turn_in[me] = turn_out[me]

    await_sides(pack_copy)
    zero_row = jnp.zeros((layers, 1, ny), jnp.float32)

    def low_of(k):
        return jnp.where(has_low, pack_in[0, k], zero_row)

    def high_of(k):
        return jnp.where(has_high, pack_in[1, k], zero_row)

    one_row = jnp.ones_like(zero_row)
    cond_b = jnp.where(has_low, pack_in[0, 0], one_row)
    cond_a = jnp.where(has_high, pack_in[1, 0], one_row)
    pres_b, pres_a = low_of(1), high_of(1)
    diag_b = jnp.where(has_low, pack_in[0, 3], one_row)
    diag_a = jnp.where(has_high, pack_in[1, 3], one_row)
    t_lo = jnp.where(has_low, harmonic(cond_b, conduct[:, 0:1]), zero_row)
    t_hi = jnp.where(has_high, harmonic(conduct[:, rows - 1 : rows], cond_a), zero_row)
    drop_b = t_lo * (pres_b - pres[:, 0:1])
    drop_a = t_hi * (pres_a - pres[:, rows - 1 : rows])
    z_b = (low_of(2) - drop_b) / (diag_b + t_lo)
    full_a = diag_a + t_hi
    z_a = (high_of(2) - drop_a) / full_a

    zero = jnp.zeros(field, jnp.float32)
    diag = diag_part + jnp.where(first_row, t_lo, zero) + jnp.where(end_row, t_hi, zero)
    res = res_part + jnp.where(first_row, drop_b, zero) + jnp.where(end_row, drop_a, zero)
    z0 = res / diag
    nz = (
        around(z0)
        + jnp.where(first_row, t_lo * z_b, zero)
        + jnp.where(end_row, t_hi * z_a, zero)
    )
    v = nz / diag
    ty_a = y_faces(cond_a)
    tz_a = z_faces(cond_a)
    nz_a = (
        t_hi * z0[:, rows - 1 : rows]
        + high_of(5) * high_of(4)
        + last_lane(ty_a) * last_lane(z_a)
        + ty_a * next_lane(z_a)
        + shift_z(tz_a, -1) * shift_z(z_a, -1)
        + tz_a * shift_z(z_a, 1)
    )
    v_a = nz_a / full_a
    tx_all = jnp.where(end_row, t_hi, tx)
    v_up = tx_all * jnp.where(end_row, v_a, next_row(v)) + ty * next_lane(v) + tz * shift_z(v, 1)

    def column(f):
        f = jnp.sum(jnp.sum(f, axis=0), axis=0, keepdims=True)
        return sum(f[:, i : i + LANES] for i in range(0, ny, LANES))

    columns = (column(res * z0), column(z0 * nz), column(v * nz), column(2.0 * (v * v_up)))
    sum_row = iota((8, LANES), 0)
    partial = jnp.zeros((8, LANES), jnp.float32)
    for k, col in enumerate(columns):
        partial = jnp.where(sum_row == k, col, partial)
    sum_out[...] = partial
    start_all(sum_copy)
    sum_in[me] = partial

    some = pl.ds(0, peers - 1)
    whole(turn_out.at[some], turn_in.at[some], turn_ss, turn_rs).wait_recv()
    await_sides(functools.partial(edge_copy, 0))
    per = LANES // rows
    blocks = [
        group_transpose([turn_in[b * per + i] for i in range(per)], rows)
        for b in range(peers // per)
    ]

    def component(c):
        def layer(z):
            parts = [block[c * layers + z] for block in blocks]
            return parts[0] if len(parts) == 1 else jnp.concatenate(parts, axis=1)

        return jnp.stack([layer(z) for z in range(layers)])

    shape = (layers, yrows, nx)
    y_first, y_end = iota(shape, 1) == 0, iota(shape, 1) == yrows - 1
    f_x = jnp.where(iota(shape, 2) == nx - 1, 0.0, component(0))
    f_y = component(1)
    f_z = jnp.where(iota(shape, 0) == layers - 1, 0.0, component(2))
    f_y_low = component(3)
    up_x, up_y, up_z, up_y_low = f_x > 0, f_y > 0, f_z > 0, f_y_low > 0
    weight = step_size / poro_ref[...]
    edge_zero = jnp.zeros((layers, 1, nx), jnp.float32)

    def advance(species, step):
        result = []
        for s in range(species_n):
            c = species[s]
            below = jnp.where(has_low, edge_in[step, 0, s], edge_zero)
            above = jnp.where(has_high, edge_in[step, 1, s], edge_zero)
            c_below = jnp.where(y_first, below, last_row(c))
            c_above = jnp.where(y_end, above, next_row(c))
            div = f_y * jnp.where(up_y, c, c_above) - f_y_low * jnp.where(up_y_low, c_below, c)
            carried = f_x * jnp.where(up_x, c, next_lane(c))
            div = div + (carried - last_lane(carried))
            carried = f_z * jnp.where(up_z, c, shift_z(c, 1))
            div = div + (carried - shift_z(carried, -1))
            react = react_ref[s, 0] * species[0]
            for t in range(1, species_n):
                react = react + react_ref[s, t] * species[t]
            result.append(c - weight * div + step_size * react)
        return result

    species = advance([conc_ref[s] for s in range(species_n)], 0)
    for s in range(species_n):
        edge_out[1, 0, s] = species[s][:, 0:1]
        edge_out[1, 1, s] = species[s][:, yrows - 1 : yrows]
    both_sides(functools.partial(edge_copy, 1))

    whole(sum_in.at[some], sum_in.at[some], sum_ss, sum_rs).wait_recv()
    total = sum_in[0]
    for i in range(1, peers):
        total = total + sum_in[i]
    total = jnp.sum(total, axis=1, keepdims=True)
    g00, g01, g11, g12 = (total[k : k + 1] for k in range(4))
    delta0 = g00 - g01
    a0 = g00 / delta0
    e0 = -g01 / delta0
    gamma1 = e0 * e0 * g00 + 2.0 * a0 * e0 * g01 + a0 * a0 * g11
    cross1 = e0 * e0 * g01 + 2.0 * a0 * e0 * g11 + a0 * a0 * g12
    beta = gamma1 / g00
    a1 = gamma1 / ((gamma1 - cross1) - beta * gamma1 / a0)
    on_z = (a0 + a1 * (e0 + beta)).reshape(1, 1, 1)
    on_v = (a1 * a0).reshape(1, 1, 1)
    pressure = pres + on_z * z0 + on_v * v
    pressure_a = pres_a + on_z * z_a + on_v * v_a
    pres_out[...] = pressure
    flux_out[0] = tx_all * (pressure - jnp.where(end_row, pressure_a, next_row(pressure)))
    flux_out[1] = ty * (pressure - next_lane(pressure))
    flux_out[2] = tz * (pressure - shift_z(pressure, 1))

    stores = [
        pltpu.make_async_copy(pres_out, pres_out_hbm, store_sem.at[0]),
        pltpu.make_async_copy(flux_out, flux_out_hbm, store_sem.at[1]),
        pltpu.make_async_copy(spec_out, spec_out_hbm, store_sem.at[2]),
    ]
    stores[0].start()
    stores[1].start()

    await_sides(functools.partial(edge_copy, 1))
    species = advance(species, 1)
    for s in range(species_n):
        spec_out[s] = species[s]
    stores[2].start()

    sent_sides(pack_copy)
    sent_sides(functools.partial(edge_copy, 0))
    sent_sides(functools.partial(edge_copy, 1))
    whole(turn_out.at[some], turn_in.at[some], turn_ss, turn_rs).wait_send()
    whole(sum_in.at[some], sum_in.at[some], sum_ss, sum_rs).wait_send()
    for store in stores:
        store.wait()


def solution(mesh):
    peers = mesh.shape["gx"]

    def step(pres, src, perm, region, factor, bound, flux, conc, poro, react):
        layers, rows, ny = pres.shape
        species_n, _, yrows, nx = conc.shape
        f32 = jnp.float32
        dma = pltpu.SemaphoreType.DMA
        hbm = pl.BlockSpec(memory_space=pltpu.HBM)
        outs = pl.pallas_call(
            functools.partial(kernel, peers),
            out_shape=(
                jax.ShapeDtypeStruct(pres.shape, f32),
                jax.ShapeDtypeStruct(flux.shape, f32),
                jax.ShapeDtypeStruct(conc.shape, f32),
            ),
            in_specs=[hbm] * 10,
            out_specs=(hbm,) * 3,
            scratch_shapes=[
                pltpu.VMEM(pres.shape, f32),
                pltpu.VMEM(pres.shape, f32),
                pltpu.VMEM(pres.shape, f32),
                pltpu.VMEM(pres.shape, jnp.int32),
                pltpu.SMEM(factor.shape, f32),
                pltpu.VMEM(pres.shape, jnp.int32),
                pltpu.VMEM(flux.shape, f32),
                pltpu.VMEM(conc.shape, f32),
                pltpu.VMEM(poro.shape, f32),
                pltpu.SMEM(react.shape, f32),
                dma((10,)),
                pltpu.VMEM(pres.shape, f32),
                pltpu.VMEM(flux.shape, f32),
                pltpu.VMEM(conc.shape, f32),
                dma((3,)),
                pltpu.VMEM((2, 6, layers, 1, ny), f32),
                pltpu.VMEM((2, 6, layers, 1, ny), f32),
                pltpu.VMEM((SUBSTEPS, 2, species_n, layers, 1, nx), f32),
                pltpu.VMEM((SUBSTEPS, 2, species_n, layers, 1, nx), f32),
                pltpu.VMEM((peers, yrows, LANES), f32),
                pltpu.VMEM((peers, yrows, LANES), f32),
                pltpu.VMEM((8, LANES), f32),
                pltpu.VMEM((peers, 8, LANES), f32),
                dma((2,)),
                dma((2,)),
                dma((SUBSTEPS, 2)),
                dma((SUBSTEPS, 2)),
                dma,
                dma,
                dma,
                dma,
            ],
            compiler_params=pltpu.CompilerParams(
                collective_id=0, has_side_effects=True, vmem_limit_bytes=VMEM_GRANT
            ),
        )(pres, src, perm, region, factor, bound, flux, conc, poro, react)
        return outs

    slab = P("ens", "gx", None)
    stacked = P(None, "ens", "gx", None)
    in_specs = (slab, slab, slab, slab, P("ens"), slab, stacked, stacked, slab, P("ens", None))
    out_specs = (slab, stacked, stacked)
    return jax.shard_map(step, mesh=mesh, in_specs=in_specs, out_specs=out_specs, check_vma=False)
```

profile of v0, /device:TPU:1, one launch (start us, length us, event | category | flops | bytes accessed | tf_op | source)
XLA Modules:
  0.0 17.3 jit_solution(17812236571913238833)
XLA Ops:
  0.6 13.3 %shard_map.121 = (f32[4,8,128]{2,1,0:T(8,128)}, f32[3,4,8,128]{3,2,1,0:T(8,128)}, f32[4,4,8,128]{3,2,1,0:T(8,128)}) custom-call(f32[4,8,128]{2,1,0:T(8,128)} %pres_hbm.1, f32[4,8,128]{2,1,0:T(8,128)} %src_hbm.1, f32[4,8,128]{2,1,0:T(8,128)} %perm_hbm.1, s32[4,8,128]{2,1,0:T(8,128)} %region_hbm.1, f32[8]{0:T(128)} %factor_hbm.1, s32[4,8,128]{2,1,0:T(8,128)} %bound_hbm.1, ...), custom_call_target="tpu_custom_call" | custom-call | tf_op jit(solution)/shard_map/pallas_call | solution.py:464
  13.9 0.0 copy-start
  13.9 1.4 %copy.16 = f32[4,8,128]{2,1,0:T(8,128)} copy(f32[4,8,128]{2,1,0:T(8,128)} %get-tuple-element.6) | data formatting | bytes 32768
  15.3 1.4 %copy.17 = f32[3,4,8,128]{3,2,1,0:T(8,128)} copy(f32[3,4,8,128]{3,2,1,0:T(8,128)} %get-tuple-element.7) | data formatting | bytes 98304
  16.7 0.0 copy-done
  16.7 0.6 %copy.18 = f32[4,4,8,128]{3,2,1,0:T(8,128)} copy(f32[4,4,8,128]{3,2,1,0:T(8,128)S(1)} %copy-done) | data formatting | bytes 131072
Async XLA Ops:
  13.9 2.8 %copy-start = (f32[4,4,8,128]{3,2,1,0:T(8,128)S(1)}, f32[4,4,8,128]{3,2,1,0:T(8,128)}, u32[]{:S(2)}) copy-start(f32[4,4,8,128]{3,2,1,0:T(8,128)} %get-tuple-element.8) | copy-start | bytes 196612
where the time goes:
time: 17.7 us; the launch traced here: 17.3 us
  Pallas kernels  13.3 us (75%)
  local copies, waits for them, and re-layouts  3.41 us (19%)
  between operations  0.65 us (4%)
    pallas_call x1, Pallas kernels, step(): pl.pallas_call(functools.partial(kernel, peers), out_shape=(jax.ShapeDtyp...  13.3 us
    unnamed x5, local copies, waits for them, and re-layouts  3.41 us

commit v1 on v0

--- a/solution.py
+++ b/solution.py
@@ -9,7 +9,7 @@
 
 SUBSTEPS = 2
 LANES = 128
-VMEM_GRANT = 60 * 1024 * 1024
+VMEM_GRANT = 24 * 1024 * 1024
 step_size = 0.5
 
 
@@ -73,9 +73,9 @@
     conc_hbm,
     poro_hbm,
     react_hbm,
-    pres_out_hbm,
-    flux_out_hbm,
-    spec_out_hbm,
+    pres_out,
+    flux_out,
+    spec_out,
     pres_ref,
     src_ref,
     perm_ref,
@@ -87,10 +87,6 @@
     poro_ref,
     react_ref,
     load_sem,
-    pres_out,
-    flux_out,
-    spec_out,
-    store_sem,
     pack_out,
     pack_in,
     edge_out,
@@ -429,27 +425,16 @@
     flux_out[1] = ty * (pressure - next_lane(pressure))
     flux_out[2] = tz * (pressure - shift_z(pressure, 1))
 
-    stores = [
-        pltpu.make_async_copy(pres_out, pres_out_hbm, store_sem.at[0]),
-        pltpu.make_async_copy(flux_out, flux_out_hbm, store_sem.at[1]),
-        pltpu.make_async_copy(spec_out, spec_out_hbm, store_sem.at[2]),
-    ]
-    stores[0].start()
-    stores[1].start()
-
     await_sides(functools.partial(edge_copy, 1))
     species = advance(species, 1)
     for s in range(species_n):
         spec_out[s] = species[s]
-    stores[2].start()
 
     sent_sides(pack_copy)
     sent_sides(functools.partial(edge_copy, 0))
     sent_sides(functools.partial(edge_copy, 1))
     whole(turn_out.at[some], turn_in.at[some], turn_ss, turn_rs).wait_send()
     whole(sum_in.at[some], sum_in.at[some], sum_ss, sum_rs).wait_send()
-    for store in stores:
-        store.wait()
 
 
 def solution(mesh):
@@ -460,7 +445,9 @@
         species_n, _, yrows, nx = conc.shape
         f32 = jnp.float32
         dma = pltpu.SemaphoreType.DMA
+        inputs = (pres, src, perm, region, factor, bound, flux, conc, poro, react)
         hbm = pl.BlockSpec(memory_space=pltpu.HBM)
+        vmem = pl.BlockSpec(memory_space=pltpu.VMEM)
         outs = pl.pallas_call(
             functools.partial(kernel, peers),
             out_shape=(
@@ -469,7 +456,7 @@
                 jax.ShapeDtypeStruct(conc.shape, f32),
             ),
             in_specs=[hbm] * 10,
-            out_specs=(hbm,) * 3,
+            out_specs=(vmem,) * 3,
             scratch_shapes=[
                 pltpu.VMEM(pres.shape, f32),
                 pltpu.VMEM(pres.shape, f32),
@@ -482,10 +469,6 @@
                 pltpu.VMEM(poro.shape, f32),
                 pltpu.SMEM(react.shape, f32),
                 dma((10,)),
-                pltpu.VMEM(pres.shape, f32),
-                pltpu.VMEM(flux.shape, f32),
-                pltpu.VMEM(conc.shape, f32),
-                dma((3,)),
                 pltpu.VMEM((2, 6, layers, 1, ny), f32),
                 pltpu.VMEM((2, 6, layers, 1, ny), f32),
                 pltpu.VMEM((SUBSTEPS, 2, species_n, layers, 1, nx), f32),
@@ -506,7 +489,7 @@
             compiler_params=pltpu.CompilerParams(
                 collective_id=0, has_side_effects=True, vmem_limit_bytes=VMEM_GRANT
             ),
-        )(pres, src, perm, region, factor, bound, flux, conc, poro, react)
+        )(*(pltpu.with_memory_space_constraint(x, pltpu.HBM) for x in inputs))
         return outs
 
     slab = P("ens", "gx", None)

time: 17.7 us -> 15.4 us (0.87)
  local copies, waits for them, and re-layouts: 3.41 us -> 1.86 us
  Pallas kernels: 13.3 us -> 12.6 us
    unnamed x5 -> x3, local copies, waits for them, and re-layouts: 3.41 us -> 1.86 us
    pallas_call x1, Pallas kernels: 13.3 us -> 12.6 us  [step(): pl.pallas_call(functools.partial(kernel, peers), out_shape=(jax.ShapeDtyp...]
where the time goes in v1:
time: 15.4 us; the launch traced here: 15.1 us
  Pallas kernels  12.6 us (82%)
  local copies, waits for them, and re-layouts  1.86 us (12%)
  between operations  0.64 us (4%)
    pallas_call x1, Pallas kernels, step(): pl.pallas_call(functools.partial(kernel, peers), out_shape=(jax.ShapeDtyp...  12.6 us
    unnamed x3, local copies, waits for them, and re-layouts  1.86 us

profile of v1, /device:TPU:1, one launch (start us, length us, event | category | flops | bytes accessed | tf_op | source)
XLA Modules:
  0.0 15.1 jit_solution(18431754511190662672)
XLA Ops:
  0.6 12.6 %shard_map.121 = (f32[4,8,128]{2,1,0:T(8,128)S(1)}, f32[3,4,8,128]{3,2,1,0:T(8,128)S(1)}, f32[4,4,8,128]{3,2,1,0:T(8,128)S(1)}) custom-call(f32[4,8,128]{2,1,0:T(8,128)} %pres_hbm.1, f32[4,8,128]{2,1,0:T(8,128)} %src_hbm.1, f32[4,8,128]{2,1,0:T(8,128)} %perm_hbm.1, s32[4,8,128]{2,1,0:T(8,128)} %region_hbm.1, f32[8]{0:T(128)} %factor_hbm.1, ...), custom_call_target="tpu_custom_call" | custom-call | tf_op jit(solution)/shard_map/pallas_call | solution.py:451
  13.3 0.6 %copy.16 = f32[4,8,128]{2,1,0:T(8,128)} copy(f32[4,8,128]{2,1,0:T(8,128)S(1)} %get-tuple-element.6) | data formatting | bytes 32768
  13.9 0.6 %copy.17 = f32[3,4,8,128]{3,2,1,0:T(8,128)} copy(f32[3,4,8,128]{3,2,1,0:T(8,128)S(1)} %get-tuple-element.7) | data formatting | bytes 98304
  14.5 0.6 %copy.18 = f32[4,4,8,128]{3,2,1,0:T(8,128)} copy(f32[4,4,8,128]{3,2,1,0:T(8,128)S(1)} %get-tuple-element.8) | data formatting | bytes 131072

commit v2 on v1

--- a/solution.py
+++ b/solution.py
@@ -116,7 +116,7 @@
         pl.semaphore_signal(barrier, inc=1, device_id={"gx": lax.rem(me + k, peers)})
         return carry
 
-    lax.fori_loop(1, peers, greet, 0)
+    lax.fori_loop(1, peers, greet, 0, unroll=peers <= 16)
 
     pairs = (
         (region_hbm, region_ref),
@@ -243,7 +243,7 @@
             copy_of(k).start()
             return carry
 
-        lax.fori_loop(1, peers, body, 0)
+        lax.fori_loop(1, peers, body, 0, unroll=peers <= 16)
 
     def both_sides(copy_of):
         @pl.when(has_low)
@@ -435,6 +435,15 @@
     sent_sides(functools.partial(edge_copy, 1))
     whole(turn_out.at[some], turn_in.at[some], turn_ss, turn_rs).wait_send()
     whole(sum_in.at[some], sum_in.at[some], sum_ss, sum_rs).wait_send()
+
+
+def write_out(a, b, c, a_out, b_out, c_out, sem):
+    pairs = ((c, c_out), (b, b_out), (a, a_out))
+    copies = [pltpu.make_async_copy(x, y, sem.at[i]) for i, (x, y) in enumerate(pairs)]
+    for copy in copies:
+        copy.start()
+    for copy in copies:
+        copy.wait()
 
 
 def solution(mesh):
@@ -490,7 +499,13 @@
                 collective_id=0, has_side_effects=True, vmem_limit_bytes=VMEM_GRANT
             ),
         )(*(pltpu.with_memory_space_constraint(x, pltpu.HBM) for x in inputs))
-        return outs
+        return pl.pallas_call(
+            write_out,
+            out_shape=tuple(jax.ShapeDtypeStruct(o.shape, f32) for o in outs),
+            in_specs=[vmem] * 3,
+            out_specs=(hbm,) * 3,
+            scratch_shapes=[dma((3,))],
+        )(*outs)
 
     slab = P("ens", "gx", None)
     stacked = P(None, "ens", "gx", None)

time: 15.4 us -> 16.8 us (1.091)
  Pallas kernels: 12.6 us -> 14.1 us
    pallas_call x0 -> x1, Pallas kernels: none -> 1.55 us  [step(): pl.pallas_call(write_out, out_shape=tuple((jax.ShapeDtypeStruct(o.shape,...]
    unnamed x3 -> x6, local copies, waits for them, and re-layouts: 1.86 us -> 1.83 us
where the time goes in v2:
time: 16.8 us; the launch traced here: 16.5 us
  Pallas kernels  14.1 us (84%)
  local copies, waits for them, and re-layouts  1.83 us (11%)
  between operations  0.65 us (4%)
    pallas_call x1, Pallas kernels, step(): pl.pallas_call(functools.partial(kernel, peers), out_shape=(jax.ShapeDtyp...  12.5 us
    unnamed x6, local copies, waits for them, and re-layouts  1.83 us
    pallas_call x1, Pallas kernels, step(): pl.pallas_call(write_out, out_shape=tuple((jax.ShapeDtypeStruct(o.shape,...  1.55 us

profile of v2, /device:TPU:1, one launch (start us, length us, event | category | flops | bytes accessed | tf_op | source)
XLA Modules:
  0.0 16.5 jit_solution(1203904282624839673)
XLA Ops:
  0.6 12.5 %shard_map.121 = (f32[4,8,128]{2,1,0:T(8,128)S(1)}, f32[3,4,8,128]{3,2,1,0:T(8,128)S(1)}, f32[4,4,8,128]{3,2,1,0:T(8,128)S(1)}) custom-call(f32[4,8,128]{2,1,0:T(8,128)} %pres_hbm.1, f32[4,8,128]{2,1,0:T(8,128)} %src_hbm.1, f32[4,8,128]{2,1,0:T(8,128)} %perm_hbm.1, s32[4,8,128]{2,1,0:T(8,128)} %region_hbm.1, f32[8]{0:T(128)} %factor_hbm.1, ...), custom_call_target="tpu_custom_call" | custom-call | tf_op jit(solution)/shard_map/pallas_call | solution.py:460
  13.2 0.0 copy-start
  13.2 0.6 %copy-done = f32[4,4,8,128]{3,2,1,0:T(8,128)} copy-done((f32[4,4,8,128]{3,2,1,0:T(8,128)}, f32[4,4,8,128]{3,2,1,0:T(8,128)S(1)}, u32[]{:S(2)}) %copy-start) | copy-done | bytes 65560
  13.8 0.0 copy-start.1
  13.8 0.6 %copy-done.1 = f32[3,4,8,128]{3,2,1,0:T(8,128)} copy-done((f32[3,4,8,128]{3,2,1,0:T(8,128)}, f32[3,4,8,128]{3,2,1,0:T(8,128)S(1)}, u32[]{:S(2)}) %copy-start.1) | copy-done | bytes 49176
  14.4 0.0 copy-start.2
  14.4 0.6 %copy-done.2 = f32[4,8,128]{2,1,0:T(8,128)} copy-done((f32[4,8,128]{2,1,0:T(8,128)}, f32[4,8,128]{2,1,0:T(8,128)S(1)}, u32[]{:S(2)}) %copy-start.2) | copy-done | bytes 16408
  15.0 1.6 %shard_map.122 = (f32[4,8,128]{2,1,0:T(8,128)}, f32[3,4,8,128]{3,2,1,0:T(8,128)}, f32[4,4,8,128]{3,2,1,0:T(8,128)}) custom-call(f32[4,8,128]{2,1,0:T(8,128)} %copy-done.2, f32[3,4,8,128]{3,2,1,0:T(8,128)} %copy-done.1, f32[4,4,8,128]{3,2,1,0:T(8,128)} %copy-done), custom_call_target="tpu_custom_call" | custom-call | tf_op jit(solution)/shard_map/pallas_call | solution.py:502
Async XLA Ops:
  13.2 0.6 %copy-start = (f32[4,4,8,128]{3,2,1,0:T(8,128)}, f32[4,4,8,128]{3,2,1,0:T(8,128)S(1)}, u32[]{:S(2)}) copy-start(f32[4,4,8,128]{3,2,1,0:T(8,128)S(1)} %get-tuple-element.8.c) | copy-start | bytes 196612
  13.8 0.6 %copy-start.1 = (f32[3,4,8,128]{3,2,1,0:T(8,128)}, f32[3,4,8,128]{3,2,1,0:T(8,128)S(1)}, u32[]{:S(2)}) copy-start(f32[3,4,8,128]{3,2,1,0:T(8,128)S(1)} %get-tuple-element.7.b) | copy-start | bytes 147460
  14.4 0.6 %copy-start.2 = (f32[4,8,128]{2,1,0:T(8,128)}, f32[4,8,128]{2,1,0:T(8,128)S(1)}, u32[]{:S(2)}) copy-start(f32[4,8,128]{2,1,0:T(8,128)S(1)} %get-tuple-element.6.a) | copy-start | bytes 49156

commit v3 on v1

--- a/solution.py
+++ b/solution.py
@@ -116,7 +116,7 @@
         pl.semaphore_signal(barrier, inc=1, device_id={"gx": lax.rem(me + k, peers)})
         return carry
 
-    lax.fori_loop(1, peers, greet, 0)
+    lax.fori_loop(1, peers, greet, 0, unroll=peers <= 16)
 
     pairs = (
         (region_hbm, region_ref),
@@ -243,7 +243,7 @@
             copy_of(k).start()
             return carry
 
-        lax.fori_loop(1, peers, body, 0)
+        lax.fori_loop(1, peers, body, 0, unroll=peers <= 16)
 
     def both_sides(copy_of):
         @pl.when(has_low)

time: 15.4 us -> 15.3 us (level)
  no operation moved by 1% of the time
where the time goes in v3:
time: 15.3 us; the launch traced here: 15 us
  Pallas kernels  12.5 us (82%)
  local copies, waits for them, and re-layouts  1.86 us (12%)
  between operations  0.64 us (4%)
    pallas_call x1, Pallas kernels, step(): pl.pallas_call(functools.partial(kernel, peers), out_shape=(jax.ShapeDtyp...  12.5 us
    unnamed x3, local copies, waits for them, and re-layouts  1.86 us

profile of v3, /device:TPU:1, one launch (start us, length us, event | category | flops | bytes accessed | tf_op | source)
XLA Modules:
  0.0 15.0 jit_solution(13784553005022231559)
XLA Ops:
  0.6 12.5 %shard_map.121 = (f32[4,8,128]{2,1,0:T(8,128)S(1)}, f32[3,4,8,128]{3,2,1,0:T(8,128)S(1)}, f32[4,4,8,128]{3,2,1,0:T(8,128)S(1)}) custom-call(f32[4,8,128]{2,1,0:T(8,128)} %pres_hbm.1, f32[4,8,128]{2,1,0:T(8,128)} %src_hbm.1, f32[4,8,128]{2,1,0:T(8,128)} %perm_hbm.1, s32[4,8,128]{2,1,0:T(8,128)} %region_hbm.1, f32[8]{0:T(128)} %factor_hbm.1, ...), custom_call_target="tpu_custom_call" | custom-call | tf_op jit(solution)/shard_map/pallas_call | solution.py:451
  13.2 0.6 %copy.16 = f32[4,8,128]{2,1,0:T(8,128)} copy(f32[4,8,128]{2,1,0:T(8,128)S(1)} %get-tuple-element.6) | data formatting | bytes 32768
  13.8 0.6 %copy.17 = f32[3,4,8,128]{3,2,1,0:T(8,128)} copy(f32[3,4,8,128]{3,2,1,0:T(8,128)S(1)} %get-tuple-element.7) | data formatting | bytes 98304
  14.4 0.6 %copy.18 = f32[4,4,8,128]{3,2,1,0:T(8,128)} copy(f32[4,4,8,128]{3,2,1,0:T(8,128)S(1)} %get-tuple-element.8) | data formatting | bytes 131072
